TPU v7x, 512 devices: a whole 4x8x8 slice. The times are simulated.
512 devices in a mesh: row: 16 (over y, x_hi), col: 32 (over x_lo, z, core).
Axes of the slice: x: 4 (x_hi: 2, x_lo: 2; x = x_hi * 2 + x_lo), y: 8, z: 8, core: 2. Of those that a mesh axis runs over, the one named last changes fastest.
Arguments:
- height: float32 [2048, 4096], P('row', 'col'), may hold values from -6 to 6
- density: float32 [2048, 4096], P('row', 'col'), may hold values from 0.2 to 1
- target: float32 [2048, 4096], P('row', 'col'), may hold values from -6 to 6
- region_of_block: int32 [16, 32], P('row', 'col'), may hold values from 0 to 127
- class_of_block: int32 [16, 32], P('row', 'col'), may hold values from 0 to 7
- fill_level: float32 [128], replicated, may hold values from 0 to 0.5
- rates: float32 [8], replicated, may hold values from 0.1 to 0.6
- col_taps: float32 [8, 33], replicated, may hold values from -1 to 1
- row_taps: float32 [8, 33], replicated, may hold values from -1 to 1
- gains: float32 [8], replicated, may hold values from 0.2 to 0.6
Outputs:
- new_height: float32 [2048, 4096], P('row', 'col')
- gain_grad: float32 [8], replicated
- fill_grad: float32 [128], replicated
All inputs are finite; a program needn't handle non-finite values.
Results may differ from a plain program's by a relative error of at most 0.00035.
The roundings to bfloat16 on the way count: a program that leaves them out, or rounds other values in their place, can miss the bound.
Values may be sent and summed in bfloat16 or wider, within the bound.
No kernel may reach another device: no remote copies, remote signals or barrier semaphores. Data moves between devices by JAX's collectives and lax.ppermute only.
A program may use at most 128 MiB of HBM per device.

v0:
```python
import jax
import jax.numpy as jnp
from jax import lax
from jax.sharding import PartitionSpec as P

CHANNELS = 8
TAPS = 33
BLOCK = 128


def kernel_table(tap_weights, length):
    table = []
    for channel in range(CHANNELS):
        grouped = {}
        ordered = []
        for position in range(TAPS):
            offset = (position - TAPS // 2) * 2**channel % length
            if offset not in grouped:
                grouped[offset] = []
                ordered.append(offset)
            grouped[offset].append(position)
        entries = []
        for offset in ordered:
            summed = jnp.zeros((), jnp.float32)
            for position in grouped[offset]:
                summed = summed + tap_weights[channel, position]
            rounded = lax.optimization_barrier(summed.astype(jnp.bfloat16)).astype(jnp.float32)
            entries.append((offset, rounded))
        table.append(entries)
    return table


def shift_sum(band, entries, first, local_len, axis, direction):
    total = band.shape[axis]
    doubled = jnp.concatenate([band, band], axis=axis)
    summed = None
    for offset, weight in entries:
        start = jnp.mod(first + direction * offset, total)
        window = lax.dynamic_slice_in_dim(doubled, start, local_len, axis)
        term = weight * window.astype(jnp.float32)
        summed = term if summed is None else summed + term
    return summed


def spread_add(placed_terms, template_shape, total, axis):
    local_len = template_shape[axis]
    wide_shape = list(template_shape)
    wide_shape[axis] = total + local_len
    running = jnp.zeros(tuple(wide_shape), jnp.float32)
    for start, contribution in placed_terms:
        window = lax.dynamic_slice_in_dim(running, start, local_len, axis)
        running = lax.dynamic_update_slice_in_dim(running, window + contribution, start, axis)
    head = lax.slice_in_dim(running, 0, local_len, axis=axis) + lax.slice_in_dim(
        running, total, total + local_len, axis=axis
    )
    middle = lax.slice_in_dim(running, local_len, total, axis=axis)
    return jnp.concatenate([head, middle], axis=axis)


def shards(
    height,
    density,
    target,
    region_of_block,
    class_of_block,
    fill_level,
    rates,
    col_taps,
    row_taps,
    gains,
):
    rows_here, cols_here = height.shape
    total_rows = rows_here * lax.axis_size("row")
    total_cols = cols_here * lax.axis_size("col")
    row_first = lax.axis_index("row") * rows_here
    col_first = lax.axis_index("col") * cols_here
    block_rows, block_cols = region_of_block.shape
    block_side = rows_here // block_rows
    region_hot = (
        region_of_block[:, :, None] == jnp.arange(fill_level.shape[0], dtype=jnp.int32)
    ).astype(jnp.float32)
    class_hot = (class_of_block[:, :, None] == jnp.arange(rates.shape[0], dtype=jnp.int32)).astype(
        jnp.float32
    )
    fill_block = jnp.sum(region_hot * fill_level, axis=2)
    rate_block = jnp.sum(class_hot * rates, axis=2)

    def to_cells(values):
        spread_out = jnp.broadcast_to(
            values[:, None, :, None], (block_rows, block_side, block_cols, block_side)
        )
        return spread_out.reshape(rows_here, cols_here)

    effective = density + to_cells(fill_block)
    rate_cells = to_cells(rate_block)
    source = (effective * height).astype(jnp.bfloat16)
    col_table = kernel_table(col_taps, total_cols)
    row_table = kernel_table(row_taps, total_rows)
    source_band = lax.all_gather(source, "col", axis=1, tiled=True)
    smoothed = jnp.stack(
        [
            shift_sum(source_band, col_table[channel], col_first, cols_here, 1, -1)
            for channel in range(CHANNELS)
        ]
    ).astype(jnp.bfloat16)
    channel_band = lax.all_gather(smoothed, "row", axis=1, tiled=True)
    pressure_arg = jnp.zeros((rows_here, cols_here), jnp.float32)
    for channel in range(CHANNELS):
        pressure_arg = pressure_arg + gains[channel] * shift_sum(
            channel_band[channel], row_table[channel], row_first, rows_here, 0, -1
        )
    shifted = 1.0 + pressure_arg
    new_height = height - rate_cells * jax.nn.softplus(shifted)
    pressure_adjoint = (
        -(new_height - target) * rate_cells * jax.nn.sigmoid(shifted) / BLOCK
    ).astype(jnp.bfloat16)
    adjoint_band = lax.all_gather(pressure_adjoint, "row", axis=0, tiled=True)
    channel_adjoint = jnp.stack(
        [
            shift_sum(adjoint_band, row_table[channel], row_first, rows_here, 0, 1)
            for channel in range(CHANNELS)
        ]
    )
    gain_local = jnp.sum(channel_adjoint * smoothed.astype(jnp.float32), axis=(1, 2))
    gain_grad = lax.psum(gain_local, ("row", "col"))
    weighted = (gains[:, None, None] * channel_adjoint).astype(jnp.bfloat16)
    placed_columns = []
    for channel in range(CHANNELS):
        channel_values = weighted[channel].astype(jnp.float32)
        for offset, weight in col_table[channel]:
            start = jnp.mod(col_first - offset, total_cols)
            placed_columns.append((start, weight * channel_values))
    column_terms = spread_add(placed_columns, (rows_here, cols_here), total_cols, 1)
    source_adjoint = lax.psum_scatter(
        column_terms.astype(jnp.bfloat16), "col", scatter_dimension=1, tiled=True
    ).astype(jnp.float32)
    block_sums = jnp.sum(
        (source_adjoint * height).reshape(block_rows, block_side, block_cols, block_side),
        axis=(1, 3),
    )
    fill_local = jnp.sum(region_hot * block_sums[:, :, None], axis=(0, 1))
    fill_grad = lax.psum(fill_local, ("row", "col"))
    return (new_height, gain_grad, fill_grad)


def solution(mesh):
    in_specs = (
        P("row", "col"),
        P("row", "col"),
        P("row", "col"),
        P("row", "col"),
        P("row", "col"),
        P(),
        P(),
        P(),
        P(),
        P(),
    )
    out_specs = (P("row", "col"), P(), P())
    return jax.shard_map(shards, mesh=mesh, in_specs=in_specs, out_specs=out_specs, check_vma=False)
```

profile of v0, /device:TPU:1, one launch (start us, length us, event | category | flops | bytes accessed | tf_op | source)
XLA Modules:
  0.0 1034.6 jit_solution(17635049522354549897)
XLA Ops:
  7.9 1.3 fusion.1270
  9.1 2.1 multiply_convert_fusion.2
  191.6 1.4 constant_dynamic-update-slice_fusion.1
  194.0 1.0 constant_dynamic-update-slice_fusion.8
  195.0 1.0 constant_dynamic-update-slice_fusion.7
  196.0 1.0 constant_dynamic-update-slice_fusion.6
  197.0 1.0 constant_dynamic-update-slice_fusion.5
  198.0 1.0 constant_dynamic-update-slice_fusion.4
  198.9 1.3 constant_dynamic-update-slice_fusion.3
  200.3 1.0 constant_dynamic-update-slice_fusion.2
  387.4 2.4 slice_bitcast_fusion.4
  389.8 0.9 fusion.1041
  390.7 0.9 fusion.1026
  392.1 0.9 fusion.1042
  393.0 1.0 fusion.1073
  394.0 0.9 fusion.1074
  394.9 0.9 fusion.1106
  395.8 0.9 fusion.1053
  396.6 0.9 fusion.1085
  397.9 0.9 fusion.1124
  398.8 0.9 fusion.1091
  399.7 0.9 fusion.1059
  400.5 0.9 fusion.1103
  401.4 0.9 fusion.1025
  402.4 0.9 fusion.1097
  403.3 0.9 fusion.1163
  404.1 0.9 fusion.1130
  405.0 1.3 fusion.1118
  406.3 0.9 fusion.1065
  407.2 0.9 fusion.1107
  411.0 89.8 %multiply_add_fusion.1 = f32[128,128]{1,0:T(8,128)S(1)} fusion(s32[]{:T(128)S(6)} %select_n.5624, bf16[2048,128]{1,0:T(8,128)(2,1)S(1)} %get-tuple-element.12, s32[]{:T(128)S(6)} %select_n.5594, s32[]{:T(128)S(6)} %select_n.5596, s32[]{:T(128)S(6)} %select_n.5598, s32[]{:T(128)S(6)} %select_n.5600, s32[]{:T(128)S(6)} %select_n.5602, s32[]{:T(128)S(6)} %select_n.5604, ...), kind=kLoop, calls=%fused_computation.2697 | loop fusion | flops 9764864 | bytes 2687446 | tf_op jit(solution)/shard_map/add | solution.py:109
  500.8 16.8 %multiply_convert_fusion.1 = (bf16[128,128]{1,0:T(8,128)(2,1)S(1)}, f32[128,128]{1,0:T(8,128)}) fusion(f32[128,128]{1,0:T(8,128)S(1)} %copy-done.5, f32[]{:T(128)} %fusion.1271, f32[128,128]{1,0:T(8,128)S(1)} %copy-done.3, bf16[128,128]{1,0:T(8,128)(2,1)S(1)} %get-tuple-element.171, f32[]{:T(128)S(6)} %convert_element_type.6866, ...), kind=kLoop, calls=%fused_computation.2693 | loop fusion | flops 8699904 | bytes 4915900 | tf_op jit(solution)/shard_map/convert_element_type | solution.py:116
  517.6 38.2 %all_gather.11 = bf16[2048,128]{1,0:T(8,128)(2,1)S(1)} all-gather(bf16[128,128]{1,0:T(8,128)(2,1)S(1)} %get-tuple-element.5), channel_id=1, replica_groups=mesh['row'=16,'col'=32] {'row'}, dimensions={0}, use_global_device_ids=true | all-gather | bytes 557056 | tf_op jit(solution)/shard_map/all_gather | solution.py:117
  556.7 0.9 bitcast_dynamic-update-slice_fusion.5
  557.6 1.0 bitcast_dynamic-update-slice_fusion.4
  558.6 0.9 bitcast_dynamic-update-slice_fusion.3
  559.5 0.9 bitcast_dynamic-update-slice_fusion.2
  560.4 0.9 bitcast_dynamic-update-slice_fusion.1
  562.9 1.0 dynamic_update_slice.789
  594.1 1.1 dynamic_update_slice.822
  625.4 1.2 dynamic_update_slice.855
  687.7 0.9 dynamic_update_slice.921
  718.3 1.1 dynamic_update_slice.954
  776.6 0.9 dynamic_update_slice.1020
  801.4 1.3 copy.13
  802.7 123.6 %reduce-scatter.4.cloned.1.call-done = bf16[128,128]{1,0:T(8,128)(2,1)} async-done(((bf16[4096,128]{1,0:T(8,128)(2,1)}), bf16[128,128]{1,0:T(8,128)(2,1)}) %reduce-scatter.4.cloned.1.call-update) | async-done | bytes 32784
  926.3 0.9 copy.14
  928.5 99.2 %all-reduce = (f32[8]{0:T(128)}, f32[128]{0:T(128)}) all-reduce(f32[8]{0:T(128)S(1)} %get-tuple-element.16, f32[128]{0:T(128)S(1)} %compare_select_fusion.2), channel_id=1, replica_groups=mesh['row'=16,'col'=32] {'row','col'}, use_global_device_ids=true, to_apply=%region_3.4 | all-reduce | flops 136 | bytes 1088 | tf_op jit(solution)/shard_map/psum | solution.py:125
  (602 shorter events, 261.5 us)
Async XLA Ops:
  7.2 6.6 copy-start.7
  7.2 184.4 %all-gather.3.cloned.1.call-start = ((), (), s32[]{:S(2)}) async-start(), calls=%async_computation.1 | async-start | bytes 1081344 | tf_op jit(solution)/shard_map/all_gather | solution.py:99
  11.3 376.1 %all-gather.5.cloned.1.call-start = ((), (), s32[]{:S(2)}) async-start(), calls=%async_computation.2 | async-start | bytes 4456448 | tf_op jit(solution)/shard_map/all_gather | solution.py:106
  191.6 1.5 copy-start
  201.2 0.7 copy-start.1
  202.0 724.3 %reduce-scatter.4.cloned.1.call-start = ((), (), s32[]{:S(2)}) async-start(), calls=%async_computation.3 | async-start | bytes 1081344
  203.8 1.9 copy-start.4
  205.1 181.0 %copy-start.8 = (f32[8]{0:T(128)S(1)}, f32[8]{0:T(128)}, u32[]{:S(2)}) copy-start(f32[8]{0:T(128)} %param.16) | copy-start | bytes 100
  205.1 181.6 %copy-start.6 = (f32[8]{0:T(128)S(1)}, f32[8]{0:T(128)}, u32[]{:S(2)}) copy-start(f32[8]{0:T(128)} %param.19) | copy-start | bytes 100
  410.2 90.5 %copy-start.3 = (f32[128,128]{1,0:T(8,128)S(1)}, f32[128,128]{1,0:T(8,128)}, u32[]{:S(2)}) copy-start(f32[128,128]{1,0:T(8,128)} %param.10) | copy-start | bytes 196612
  410.2 90.5 %copy-start.5 = (f32[128,128]{1,0:T(8,128)S(1)}, f32[128,128]{1,0:T(8,128)}, u32[]{:S(2)}) copy-start(f32[128,128]{1,0:T(8,128)} %param.12) | copy-start | bytes 196612
  559.5 3.0 copy-start.2
Sparse Core Ops, SparseCore 0:
  11.4 71.6 all-gather.2
  202.1 107.3 all-gather.4
  802.8 123.4 reduce-scatter.3
where the time goes:
time: 1050 us; the launch traced here: 1030 us
  between operations  361 us (34%)
  local copies, waits for them, and re-layouts  242 us (23%)
  other arithmetic  170 us (16%)
  blocking collectives  137 us (13%)
  waiting for transfers between devices  124 us (12%)
    dynamic_update_slice x263, local copies, waits for them, and re-layouts, spread_add(): lax.dynamic_update_slice_in_dim(running, window + contribution, start, axis)  210 us
    unnamed x4, waiting for transfers between devices  124 us
    psum x1, blocking collectives, shards(): gain_grad = lax.psum(gain_local, ('row', 'col'))  99.2 us
    add x1, other arithmetic, shards(): pressure_arg + gains[channel] * shift_sum(channel_band[channel], row_tabl...  89.8 us
    all_gather x1, blocking collectives, shards(): adjoint_band = lax.all_gather(pressure_adjoint, 'row', axis=0, tiled=True)  38.2 us
    add x262, other arithmetic, spread_add(): window + contribution  24.3 us
    slice x31, local copies, waits for them, and re-layouts, kernel_table(): summed = summed + tap_weights[channel, position]  22.2 us
  transfers between devices with their start and end apart: 3, of which 1 were waited for; matrix products, arithmetic and copies ran while one was open for 2% of the time, Pallas kernels for 0%

commit v1 on v0

--- a/solution.py
+++ b/solution.py
@@ -122,7 +122,7 @@
         ]
     )
     gain_local = jnp.sum(channel_adjoint * smoothed.astype(jnp.float32), axis=(1, 2))
-    gain_grad = lax.psum(gain_local, ("row", "col"))
+    gain_grad = lax.psum(lax.psum(gain_local, "col"), "row")
     weighted = (gains[:, None, None] * channel_adjoint).astype(jnp.bfloat16)
     placed_columns = []
     for channel in range(CHANNELS):

time: 1050 us -> 1050 us (level)
  blocking collectives: 137 us -> 234 us
  waiting for transfers between devices: 124 us -> 28.3 us
    psum x1 -> x3, blocking collectives: 99.2 us -> 196 us  [the longest x1 99.7 us: shards(): fill_grad = lax.psum(fill_local, ('row', 'col'))]
    unnamed x4, waiting for transfers between devices: 124 us -> 28.2 us
where the time goes in v1:
time: 1050 us; the launch traced here: 1030 us
  between operations  360 us (34%)
  local copies, waits for them, and re-layouts  242 us (23%)
  blocking collectives  234 us (22%)
  other arithmetic  170 us (16%)
  waiting for transfers between devices  28.3 us (3%)
    dynamic_update_slice x263, local copies, waits for them, and re-layouts, spread_add(): lax.dynamic_update_slice_in_dim(running, window + contribution, start, axis)  210 us
    psum x1, blocking collectives, shards(): fill_grad = lax.psum(fill_local, ('row', 'col'))  99.7 us
    psum x2, blocking collectives, shards(): gain_grad = lax.psum(lax.psum(gain_local, 'col'), 'row')  95.8 us
    add x1, other arithmetic, shards(): pressure_arg + gains[channel] * shift_sum(channel_band[channel], row_tabl...  89.8 us
    all_gather x1, blocking collectives, shards(): adjoint_band = lax.all_gather(pressure_adjoint, 'row', axis=0, tiled=True)  38.1 us
    unnamed x4, waiting for transfers between devices  28.2 us
    add x262, other arithmetic, spread_add(): window + contribution  24.3 us
    slice x31, local copies, waits for them, and re-layouts, kernel_table(): summed = summed + tap_weights[channel, position]  22.2 us
  transfers between devices with their start and end apart: 3, of which 1 were waited for; matrix products, arithmetic and copies ran while one was open for 2% of the time, Pallas kernels for 0%

profile of v1, /device:TPU:1, one launch (start us, length us, event | category | flops | bytes accessed | tf_op | source)
XLA Modules:
  0.0 1033.9 jit_solution(12319519080617623031)
XLA Ops:
  7.9 1.3 fusion.1270
  9.1 2.1 multiply_convert_fusion.2
  190.6 1.4 constant_dynamic-update-slice_fusion.1
  193.0 1.0 constant_dynamic-update-slice_fusion.8
  194.0 1.0 constant_dynamic-update-slice_fusion.7
  195.0 1.0 constant_dynamic-update-slice_fusion.6
  195.9 1.0 constant_dynamic-update-slice_fusion.5
  196.9 1.0 constant_dynamic-update-slice_fusion.4
  197.9 1.3 constant_dynamic-update-slice_fusion.3
  199.3 1.0 constant_dynamic-update-slice_fusion.2
  386.0 2.4 slice_bitcast_fusion.4
  388.5 0.9 fusion.1041
  389.3 0.9 fusion.1026
  390.7 0.9 fusion.1042
  391.6 1.0 fusion.1073
  392.7 0.9 fusion.1074
  393.5 0.9 fusion.1106
  394.4 0.9 fusion.1053
  395.3 0.9 fusion.1085
  396.5 0.9 fusion.1124
  397.4 0.9 fusion.1091
  398.3 0.9 fusion.1059
  399.1 0.9 fusion.1103
  400.0 0.9 fusion.1025
  401.0 0.9 fusion.1097
  401.9 0.9 fusion.1163
  402.8 0.9 fusion.1130
  403.6 1.3 fusion.1118
  404.9 0.9 fusion.1065
  409.6 89.8 %multiply_add_fusion.1 = f32[128,128]{1,0:T(8,128)S(1)} fusion(s32[]{:T(128)S(6)} %select_n.5624, bf16[2048,128]{1,0:T(8,128)(2,1)S(1)} %get-tuple-element.10, s32[]{:T(128)S(6)} %select_n.5594, s32[]{:T(128)S(6)} %select_n.5596, s32[]{:T(128)S(6)} %select_n.5598, s32[]{:T(128)S(6)} %select_n.5600, s32[]{:T(128)S(6)} %select_n.5602, s32[]{:T(128)S(6)} %select_n.5604, ...), kind=kLoop, calls=%fused_computation.2697 | loop fusion | flops 9764864 | bytes 2687446 | tf_op jit(solution)/shard_map/add | solution.py:109
  499.5 16.6 %multiply_convert_fusion.1 = (bf16[128,128]{1,0:T(8,128)(2,1)S(1)}, f32[128,128]{1,0:T(8,128)}) fusion(f32[128,128]{1,0:T(8,128)S(1)} %copy-done.5, f32[]{:T(128)} %fusion.1271, f32[128,128]{1,0:T(8,128)S(1)} %copy-done.3, bf16[128,128]{1,0:T(8,128)(2,1)S(1)} %get-tuple-element.169, f32[]{:T(128)S(6)} %convert_element_type.6866, ...), kind=kLoop, calls=%fused_computation.2693 | loop fusion | flops 8699904 | bytes 4915900 | tf_op jit(solution)/shard_map/convert_element_type | solution.py:116
  516.1 38.1 %all_gather.11 = bf16[2048,128]{1,0:T(8,128)(2,1)S(1)} all-gather(bf16[128,128]{1,0:T(8,128)(2,1)S(1)} %get-tuple-element.3), channel_id=1, replica_groups=mesh['row'=16,'col'=32] {'row'}, dimensions={0}, use_global_device_ids=true | all-gather | bytes 557056 | tf_op jit(solution)/shard_map/all_gather | solution.py:117
  555.1 0.9 bitcast_dynamic-update-slice_fusion.5
  556.0 1.0 bitcast_dynamic-update-slice_fusion.4
  557.0 0.9 bitcast_dynamic-update-slice_fusion.3
  557.9 0.9 bitcast_dynamic-update-slice_fusion.2
  558.8 0.9 bitcast_dynamic-update-slice_fusion.1
  561.3 1.0 dynamic_update_slice.789
  592.5 1.1 dynamic_update_slice.822
  623.8 1.2 dynamic_update_slice.855
  686.2 0.9 dynamic_update_slice.921
  716.7 1.1 dynamic_update_slice.954
  775.0 0.9 dynamic_update_slice.1020
  799.8 1.3 copy.13
  801.1 65.6 %psum.21 = f32[8]{0:T(128)S(1)} all-reduce(f32[8]{0:T(128)S(1)} %get-tuple-element.14), channel_id=1, replica_groups=mesh['row'=16,'col'=32] {'col'}, use_global_device_ids=true, to_apply=%region_3.4 | all-reduce | flops 8 | bytes 64 | tf_op jit(solution)/shard_map/psum | solution.py:125
  866.7 30.3 %psum.22 = f32[8]{0:T(128)} all-reduce(f32[8]{0:T(128)S(1)} %psum.21), channel_id=1, replica_groups=mesh['row'=16,'col'=32] {'row'}, use_global_device_ids=true, to_apply=%region_4.5 | all-reduce | flops 8 | bytes 64 | tf_op jit(solution)/shard_map/psum | solution.py:125
  896.9 28.2 %reduce-scatter.4.cloned.1.call-done = bf16[128,128]{1,0:T(8,128)(2,1)} async-done(((bf16[4096,128]{1,0:T(8,128)(2,1)}), bf16[128,128]{1,0:T(8,128)(2,1)}) %reduce-scatter.4.cloned.1.call-update) | async-done | bytes 32784
  927.3 99.7 %psum.23 = f32[128]{0:T(128)} all-reduce(f32[128]{0:T(128)S(1)} %compare_select_fusion.2), channel_id=1, replica_groups=mesh['row'=16,'col'=32] {'row','col'}, use_global_device_ids=true, to_apply=%region_7.8 | all-reduce | flops 128 | bytes 1024 | tf_op jit(solution)/shard_map/psum | solution.py:142
  (604 shorter events, 263.2 us)
Async XLA Ops:
  7.2 6.6 copy-start.7
  7.2 183.4 %all-gather.3.cloned.1.call-start = ((), (), s32[]{:S(2)}) async-start(), calls=%async_computation.1 | async-start | bytes 1081344 | tf_op jit(solution)/shard_map/all_gather | solution.py:99
  11.3 374.7 %all-gather.5.cloned.1.call-start = ((), (), s32[]{:S(2)}) async-start(), calls=%async_computation.2 | async-start | bytes 4456448 | tf_op jit(solution)/shard_map/all_gather | solution.py:106
  190.6 1.5 copy-start
  200.2 0.7 copy-start.1
  201.0 724.2 %reduce-scatter.4.cloned.1.call-start = ((), (), s32[]{:S(2)}) async-start(), calls=%async_computation.3 | async-start | bytes 1081344
  202.8 1.9 copy-start.4
  204.1 180.7 %copy-start.8 = (f32[8]{0:T(128)S(1)}, f32[8]{0:T(128)}, u32[]{:S(2)}) copy-start(f32[8]{0:T(128)} %param.16) | copy-start | bytes 100
  204.1 181.3 %copy-start.6 = (f32[8]{0:T(128)S(1)}, f32[8]{0:T(128)}, u32[]{:S(2)}) copy-start(f32[8]{0:T(128)} %param.19) | copy-start | bytes 100
  408.8 90.6 %copy-start.3 = (f32[128,128]{1,0:T(8,128)S(1)}, f32[128,128]{1,0:T(8,128)}, u32[]{:S(2)}) copy-start(f32[128,128]{1,0:T(8,128)} %param.10) | copy-start | bytes 196612
  408.8 90.6 %copy-start.5 = (f32[128,128]{1,0:T(8,128)S(1)}, f32[128,128]{1,0:T(8,128)}, u32[]{:S(2)}) copy-start(f32[128,128]{1,0:T(8,128)} %param.12) | copy-start | bytes 196612
  557.9 3.0 copy-start.2
Sparse Core Ops, SparseCore 0:
  11.4 71.6 all-gather.2
  201.1 107.4 all-gather.4
  801.2 123.8 reduce-scatter.3
